TPU v7x, 128 devices: a whole 4x4x4 slice. The times are simulated.
128 devices in a mesh: occ: 16 (over y, z), vir: 8 (over x, core).
Axes of the slice: x: 4, y: 4, z: 4, core: 2. Of those that a mesh axis runs over, the one named last changes fastest.
Arguments:
- amplitudes: bfloat16 [256, 8, 64, 4096], P(('occ', 'vir')), may hold values from -6 to 6
- tile_counts: int32 [256], P(('occ', 'vir')), may hold values from 1 to 8, 1536 in all
- tile_owner: int32 [256, 8], P(('occ', 'vir')), may hold values from 0 to 15, all different within a row; in each aligned block of 2 rows (0 to 1, 2 to 3, ...) at most 2 rows name the same one
- tile_local: int32 [256, 8], P(('occ', 'vir')), may hold values from 0 to 15
- pair_map: int32 [256], replicated, may hold values from 0 to 255, each once
- hole_weight: bfloat16 [256, 64, 64], P(('occ', 'vir')), may hold values from -0.75 to 0.75
- fock_tiles: bfloat16 [16, 64, 64], replicated, may hold values from -0.75 to 0.75
- ladder_panels: bfloat16 [256, 4096, 128], P('occ', 'vir'), may hold values from -0.03125 to 0.03125
Outputs:
- local_residual: bfloat16 [256, 8, 64, 4096], P(('occ', 'vir'))
- ladder_panel: bfloat16 [256, 64, 128], P(('occ', 'vir'))
Inputs may be any that keep to these rules, and one draw needn't show every extreme that they name: `tile_counts`: entries of a list at or past its count are not used. `tile_owner`: the 8 entries of a pair tile name different owners; among the pair tiles of one device no owner is named by more than 2 entries. `pair_map`: every virtual tile pair stands at exactly one owner position.
All inputs are finite; a program needn't handle non-finite values. No bound on the sum of `tile_counts` on one device may be relied on, other than what follows from the above.
Results may differ from a plain program's by a relative error of at most 0.001.
Values may be sent and summed in bfloat16 or wider, within the bound.
A program may use at most 320 MiB of HBM per device.

v0:
```python
import jax
import jax.numpy as jnp
from jax import lax
from jax.sharding import PartitionSpec as P

CAP = 2


def per_device(
    amplitudes,
    tile_counts,
    tile_owner,
    tile_local,
    pair_map,
    hole_weight,
    fock_tiles,
    ladder_panels,
):
    owners = lax.axis_size("occ")
    per_owner = ladder_panels.shape[0]
    panel_width = ladder_panels.shape[2]
    tile_count = fock_tiles.shape[0]
    tile_width = fock_tiles.shape[1]
    local_tiles, slot_count, pair_rows, tile_size = amplitudes.shape
    whole_tiles = pair_map.shape[0]
    used_slot = jnp.arange(slot_count, dtype=jnp.int32)[None, :] < tile_counts[:, None]
    tile_pos = tile_owner * per_owner + tile_local
    flat_owner = tile_owner.reshape(-1)
    owner_hits = (flat_owner[:, None] == jnp.arange(owners, dtype=jnp.int32)[None, :]).astype(
        jnp.int32
    )
    earlier = jnp.cumsum(owner_hits, axis=0) - owner_hits
    slot_rank = jnp.sum(earlier * owner_hits, axis=1)
    send_index = flat_owner * CAP + slot_rank
    kept = jnp.where(used_slot[:, :, None, None], amplitudes, jnp.zeros((), jnp.bfloat16))
    kept = kept.reshape(local_tiles * slot_count, pair_rows, tile_size)
    outgoing = (
        jnp.zeros((owners * CAP, pair_rows, tile_size), jnp.bfloat16).at[send_index].set(kept)
    )
    outgoing = outgoing.reshape(owners, CAP, pair_rows, tile_size)
    marked = jnp.where(used_slot, tile_local, -1).reshape(-1)
    out_slot = (
        jnp.full((owners * CAP,), -1, jnp.int32).at[send_index].set(marked).reshape(owners, CAP)
    )
    arrived, arrived_slot = (
        lax.all_to_all(outgoing, "occ", split_axis=0, concat_axis=0, tiled=True),
        lax.all_to_all(out_slot, "occ", split_axis=0, concat_axis=0, tiled=True),
    )
    selector = (
        arrived_slot[:, :, None] == jnp.arange(per_owner, dtype=jnp.int32)[None, None, :]
    ).astype(jnp.bfloat16)
    chosen = jnp.einsum(
        "ock,knq->ocnq",
        selector,
        lax.all_gather(ladder_panels, "vir", axis=1, tiled=True),
        preferred_element_type=jnp.float32,
    ).astype(jnp.bfloat16)
    partial_value = jnp.einsum(
        "ocpn,ocnq->ocpq", arrived, chosen, preferred_element_type=jnp.float32
    )
    returned = lax.all_to_all(partial_value, "occ", split_axis=0, concat_axis=0, tiled=True)
    match_pos = tile_pos[:, :, None] == jnp.arange(whole_tiles, dtype=jnp.int32)[None, None, :]
    tile_ident = jnp.sum(jnp.where(match_pos, pair_map[None, None, :], 0), axis=2)
    tile_range = jnp.arange(tile_count, dtype=jnp.int32)[None, None, :]
    pick_rows = ((tile_ident // tile_count)[:, :, None] == tile_range).astype(jnp.bfloat16)
    pick_cols = ((tile_ident % tile_count)[:, :, None] == tile_range).astype(jnp.bfloat16)
    left_fock = jnp.einsum(
        "Psn,nce->Psce", pick_rows, fock_tiles, preferred_element_type=jnp.float32
    ).astype(jnp.bfloat16)
    right_fock = jnp.einsum(
        "Psn,nce->Psce", pick_cols, fock_tiles, preferred_element_type=jnp.float32
    ).astype(jnp.bfloat16)
    hole = jnp.einsum("Ppq,Psqx->Pspx", hole_weight, amplitudes, preferred_element_type=jnp.float32)
    shaped = amplitudes.reshape(local_tiles, slot_count, pair_rows, tile_width, tile_width)
    fock_part = jnp.einsum(
        "Pspce,Psed->Pspcd", shaped, right_fock, preferred_element_type=jnp.float32
    )
    fock_part = fock_part + jnp.einsum(
        "Psce,Psped->Pspcd", left_fock, shaped, preferred_element_type=jnp.float32
    )
    summed = hole + fock_part.reshape(local_tiles, slot_count, pair_rows, tile_size)
    local_residual = jnp.where(used_slot[:, :, None, None], summed, 0.0).astype(jnp.bfloat16)
    flat_back = returned.reshape(owners * CAP, pair_rows, panel_width)
    per_slot = flat_back[send_index].reshape(local_tiles, slot_count, pair_rows, panel_width)
    ladder_panel = jnp.sum(jnp.where(used_slot[:, :, None, None], per_slot, 0.0), axis=1).astype(
        jnp.bfloat16
    )
    return (local_residual, ladder_panel)


def solution(mesh):
    in_specs = (
        P(("occ", "vir"), None, None, None),
        P(("occ", "vir")),
        P(("occ", "vir"), None),
        P(("occ", "vir"), None),
        P(),
        P(("occ", "vir"), None, None),
        P(),
        P("occ", "vir", None),
    )
    out_specs = (P(("occ", "vir"), None, None, None), P(("occ", "vir"), None, None))
    return jax.shard_map(
        per_device, mesh=mesh, in_specs=in_specs, out_specs=out_specs, check_vma=False
    )
```

profile of v0, /device:TPU:1, one launch (start us, length us, event | category | flops | bytes accessed | tf_op | source)
XLA Modules:
  0.0 427.3 jit_solution(15080967859774291361)
XLA Ops:
  7.2 4.2 copy.46
  11.5 0.8 eq.80
  12.3 0.8 broadcast_select_fusion.1
  13.5 0.6 scatter_custom_fusion.1
  14.1 0.7 all_to_all.13
  14.8 8.6 %all-to-all-start.1 = ((s32[16,1,2]{2,1,0:T(1,128)}), s32[16,1,2]{2,1,0:T(1,128)S(1)}, u32[]{:S(2)}, u32[]{:S(2)}) async-start(s32[16,1,2]{2,1,0:T(1,128)} %bitcast.17), calls=%async_computation.1 | async-start | bytes 16384 | tf_op jit(solution)/shard_map/all_to_all | solution.py:47
  23.4 0.7 iota_compare_fusion.5
  24.2 8.5 %broadcast_select_fusion = bf16[2,8,64,4096]{3,2,1,0:T(8,128)(2,1)} fusion(bf16[2,8,64,4096]{3,2,1,0:T(8,128)(2,1)} %param.8, pred[2,8]{1,0:T(4,128)(4,1)S(1)} %iota_compare_fusion.5), kind=kLoop, calls=%fused_computation.11 | loop fusion | flops 4194304 | bytes 16777232 | tf_op jit(solution)/shard_map/jit(_where)/select_n | solution.py:35
  32.6 6.0 %broadcast_in_dim.76 = bf16[32,64,4096]{2,1,0:T(8,128)(2,1)} broadcast(bf16[]{:T(256)} %constant.43.clone.1), dimensions={} | broadcast | bytes 16777218 | tf_op jit(solution)/shard_map/broadcast_in_dim | solution.py:38
  38.6 22.0 %scatter_fusion = bf16[32,64,4096]{2,1,0:T(8,128)(2,1)} fusion(bf16[32,64,4096]{2,1,0:T(8,128)(2,1)} %broadcast_in_dim.76, s32[16]{0:T(128)S(1)} %fusion.25, bf16[16,64,4096]{2,1,0:T(8,128)(2,1)} %bitcast.65), kind=kCustom, calls=%fused_computation.1 | custom fusion | bytes 25165888 | tf_op jit(solution)/shard_map/scatter | solution.py:38
  60.6 6.8 %all-to-all-start = ((bf16[16,2,64,4096]{3,2,1,0:T(8,128)(2,1)}), bf16[16,2,64,4096]{3,2,1,0:T(8,128)(2,1)}, u32[]{:S(2)}, u32[]{:S(2)}) async-start(bf16[16,2,64,4096]{3,2,1,0:T(8,128)(2,1)} %bitcast.64), calls=%async_computation | async-start | bytes 33554432 | tf_op jit(solution)/shard_map/all_to_all | solution.py:46
  67.4 23.7 %reshape.114 = bf16[2,8,64,64,64]{4,3,2,1,0:T(8,128)(2,1)} reshape(bf16[2,8,64,4096]{3,2,1,0:T(8,128)(2,1)} %param.8) | data formatting | bytes 16777216 | tf_op jit(solution)/shard_map/reshape | solution.py:74
  92.0 24.2 %fusion.8 = f32[2,8,64,64,64]{4,2,3,1,0:T(8,128)} fusion(bf16[2,8,64,64,64]{4,3,2,1,0:T(8,128)(2,1)} %reshape.114, bf16[2,8,64,64,1]{3,1,2,0,4:T(8,128)(2,1)S(1)} %fusion.5), kind=kOutput, calls=%fused_computation.18 | convolution fusion | flops 536870912 | bytes 25296896 | tf_op jit(solution)/shard_map/Pspce,Psed->Pspcd/dot_general | solution.py:75
  116.2 28.8 %bitcast_add_fusion = f32[2,8,64,64,64]{3,4,2,1,0:T(8,128)} fusion(f32[2,8,64,64,64]{4,2,3,1,0:T(8,128)} %fusion.8, bf16[2,8,64,64,64]{4,3,2,1,0:T(8,128)(2,1)} %reshape.114, bf16[2,8,64,64,1]{3,1,2,0,4:T(8,128)(2,1)S(1)} %fusion.6), kind=kOutput, calls=%fused_computation.3 | convolution fusion | flops 541065216 | bytes 42074112 | tf_op jit(solution)/shard_map/Psce,Psped->Pspcd/dot_general | solution.py:78
  145.0 31.1 %copy.43 = f32[2,8,64,64,64]{4,3,2,1,0:T(8,128)} copy(f32[2,8,64,64,64]{3,4,2,1,0:T(8,128)} %bitcast_add_fusion) | data formatting | bytes 33554432 | tf_op jit(solution)/shard_map/add | solution.py:78
  176.1 27.9 %reshape.115 = f32[2,8,64,4096]{3,2,1,0:T(8,128)} reshape(f32[2,8,64,64,64]{4,3,2,1,0:T(8,128)} %copy.43) | data formatting | bytes 33554432 | tf_op jit(solution)/shard_map/reshape | solution.py:81
  204.0 23.1 %convolution_convert_fusion = bf16[16,2,4096,128]{3,0,2,1:T(8,128)(2,1)} fusion(bf16[16,4096,128]{2,0,1:T(8,128)(2,1)} %all-gather.2.cloned.1.call-done, s32[16,2]{0,1:T(2,128)S(1)} %bitcast.67), kind=kOutput, calls=%fused_computation.6 | convolution fusion | flops 553648640 | bytes 50331776 | tf_op jit(solution)/shard_map/ock,knq->ocnq/dot_general | solution.py:52
  227.2 132.5 %all-to-all-done = bf16[16,2,64,4096]{3,2,1,0:T(8,128)(2,1)} async-done(((bf16[16,2,64,4096]{3,2,1,0:T(8,128)(2,1)}), bf16[16,2,64,4096]{3,2,1,0:T(8,128)(2,1)}, u32[]{:S(2)}, u32[]{:S(2)}) %all-to-all-start) | async-done | bytes 16777248 | tf_op jit(solution)/shard_map/all_to_all | solution.py:46
  359.7 32.5 %fusion = f32[16,2,64,128]{3,2,1,0:T(8,128)} fusion(bf16[16,2,64,4096]{3,2,1,0:T(8,128)(2,1)} %all-to-all-done, bf16[16,2,4096,128]{3,0,2,1:T(8,128)(2,1)} %convolution_convert_fusion), kind=kOutput, calls=%fused_computation.4 | convolution fusion | flops 2147483648 | bytes 51380224 | tf_op jit(solution)/shard_map/ocpn,ocnq->ocpq/dot_general | solution.py:58
  392.2 12.6 %all-to-all-start.2 = ((f32[16,2,64,128]{3,2,1,0:T(8,128)}), f32[16,2,64,128]{3,2,1,0:T(8,128)S(1)}, u32[]{:S(2)}, u32[]{:S(2)}) async-start(f32[16,2,64,128]{3,2,1,0:T(8,128)} %fusion), calls=%async_computation.2 | async-start | bytes 2097152 | tf_op jit(solution)/shard_map/all_to_all | solution.py:61
  404.9 13.9 %fusion.4 = bf16[2,8,64,4096]{3,2,1,0:T(8,128)(2,1)} fusion(f32[2,8,64,4096]{3,2,1,0:T(8,128)} %reshape.115, bf16[2,8,64,4096]{3,2,1,0:T(8,128)(2,1)} %param.8, pred[2,8]{1,0:T(4,128)(4,1)S(1)} %iota_compare_fusion.5, bf16[2,64,64]{2,1,0:T(8,128)(2,1)S(1)} %copy-done), kind=kOutput, calls=%fused_computation.10 | convolution fusion | flops 549453824 | bytes 33570832 | tf_op jit(solution)/shard_map/Ppq,Psqx->Pspx/dot_general | solution.py:73
  418.8 0.4 all-to-all-done.2
  419.1 0.6 gather_fusion
  419.7 0.7 select_reduce_fusion
  (22 shorter events, 1.4 us)
Async XLA Ops:
  7.2 397.7 %copy-start = (bf16[2,64,64]{2,1,0:T(8,128)(2,1)S(1)}, bf16[2,64,64]{2,1,0:T(8,128)(2,1)}, u32[]{:S(2)}) copy-start(bf16[2,64,64]{2,1,0:T(8,128)(2,1)} %param.13) | copy-start | bytes 49156
  7.2 196.9 %all-gather.2.cloned.1.call-start = ((), (), s32[]{:S(2)}) async-start(), calls=%async_computation.3 | async-start | bytes 18874368 | tf_op jit(solution)/shard_map/all_gather | solution.py:55
  14.8 45.8 %all-to-all-start.1 = ((s32[16,1,2]{2,1,0:T(1,128)}), s32[16,1,2]{2,1,0:T(1,128)S(1)}, u32[]{:S(2)}, u32[]{:S(2)}) async-start(s32[16,1,2]{2,1,0:T(1,128)} %bitcast.17), calls=%async_computation.1 | async-start | bytes 16384 | tf_op jit(solution)/shard_map/all_to_all | solution.py:47
  60.6 299.1 %all-to-all-start = ((bf16[16,2,64,4096]{3,2,1,0:T(8,128)(2,1)}), bf16[16,2,64,4096]{3,2,1,0:T(8,128)(2,1)}, u32[]{:S(2)}, u32[]{:S(2)}) async-start(bf16[16,2,64,4096]{3,2,1,0:T(8,128)(2,1)} %bitcast.64), calls=%async_computation | async-start | bytes 33554432 | tf_op jit(solution)/shard_map/all_to_all | solution.py:46
  67.4 23.7 %copy-start.2 = (s32[256]{0:T(256)S(1)}, s32[256]{0:T(256)}, u32[]{:S(2)}) copy-start(s32[256]{0:T(256)} %param.12) | copy-start | bytes 3076
  67.4 23.9 %copy-start.1 = (bf16[16,64,64]{2,1,0:T(8,128)(2,1)S(1)}, bf16[16,64,64]{2,1,0:T(8,128)(2,1)}, u32[]{:S(2)}) copy-start(bf16[16,64,64]{2,1,0:T(8,128)(2,1)} %param.14) | copy-start | bytes 393220
  392.2 26.9 %all-to-all-start.2 = ((f32[16,2,64,128]{3,2,1,0:T(8,128)}), f32[16,2,64,128]{3,2,1,0:T(8,128)S(1)}, u32[]{:S(2)}, u32[]{:S(2)}) async-start(f32[16,2,64,128]{3,2,1,0:T(8,128)} %fusion), calls=%async_computation.2 | async-start | bytes 2097152 | tf_op jit(solution)/shard_map/all_to_all | solution.py:61
Sparse Core Ops, SparseCore 0:
  11.6 88.5 all-gather.1
where the time goes:
time: 432 us; the launch traced here: 427 us
  waiting for transfers between devices  133 us (31%)
  matrix products  123 us (28%)
  local copies, waits for them, and re-layouts  118 us (27%)
  starting transfers between devices  28 us (6%)
  between operations  14.1 us (3%)
  other arithmetic  11.3 us (3%)
    all_to_all x1, waiting for transfers between devices, per_device(): lax.all_to_all(outgoing, 'occ', split_axis=0, concat_axis=0, tiled=True)  133 us
    dot_general x1, matrix products, per_device(): jnp.einsum('ocpn,ocnq->ocpq', arrived, chosen, preferred_element_type=jnp...  32.5 us
    add x1, local copies, waits for them, and re-layouts, per_device(): fock_part + jnp.einsum('Psce,Psped->Pspcd', left_fock, shaped, preferred_...  31.1 us
    dot_general x1, matrix products, per_device(): jnp.einsum('Psce,Psped->Pspcd', left_fock, shaped, preferred_element_type...  28.8 us
    reshape x1, local copies, waits for them, and re-layouts, per_device(): fock_part.reshape(local_tiles, slot_count, pair_rows, tile_size)  27.9 us
    dot_general x1, matrix products, per_device(): jnp.einsum('Pspce,Psed->Pspcd', shaped, right_fock, preferred_element_typ...  24.2 us
    reshape x1, local copies, waits for them, and re-layouts, per_device(): amplitudes.reshape(local_tiles, slot_count, pair_rows, tile_width, tile_w...  23.7 us
    dot_general x1, matrix products, per_device(): jnp.einsum('ock,knq->ocnq', selector, lax.all_gather(ladder_panels, 'vir'...  23.1 us
  transfers between devices with their start and end apart: 4, of which 2 were waited for; matrix products, arithmetic and copies ran while one was open for 50% of the time, Pallas kernels for 0%

commit v1 on v0

v1 whole, which is shorter than its diff:
```python
import functools

import jax
import jax.numpy as jnp
from jax import lax
from jax.experimental import pallas as pl
from jax.experimental.pallas import tpu as pltpu
from jax.sharding import PartitionSpec as P

MESH = pl.DeviceIdType.MESH
SIDE = 4
BF16, F32, I32 = jnp.bfloat16, jnp.float32, jnp.int32
HOPS = (1, 3, 2, 0)


def body(
    counts_ref,
    owner_ref,
    local_ref,
    map_ref,
    amp_ref,
    hole_ref,
    fock_ref,
    panel_ref,
    res_ref,
    lad_ref,
    amp_vm,
    out_vm,
    arrived,
    panels,
    meta_vm,
    meta_in,
    meta_sm,
    part,
    part_in,
    ring_sum,
    home_in,
    fock_right,
    fock_left,
    spread,
    turned,
    amp_sem,
    out_sem,
    send_sem,
    arrive_sem,
    meta_send,
    meta_sem,
    panel_send,
    panel_own,
    panel_first,
    panel_second,
    part_send,
    part_sem,
    home_send,
    home_sem,
):
    tiles, slots, rows, width = amp_ref.shape
    per_owner = panel_ref.shape[0]
    side = fock_ref.shape[1]
    cols = 128
    occ, vir = lax.axis_index("occ"), lax.axis_index("vir")
    y, z = occ // SIDE, occ % SIDE
    x, c = vir // 2, vir % 2
    w = jnp.where(c == 0, z, y)
    u = jnp.where(c == 0, y, z)

    def at(xx, ww, uu, core):
        own = jnp.where(core == 0, uu * SIDE + ww, ww * SIDE + uu)
        return (own, xx * 2 + core)

    def ring(v, d):
        return lax.rem(v + d + SIDE, SIDE)

    barrier = pltpu.get_barrier_semaphore()
    greeted = 0
    for dx in range(SIDE):
        for dw in range(SIDE):
            for dc in range(2):
                if (dx, dw, dc) != (0, 0, 0):
                    cc = lax.rem(c + dc, 2)
                    own = jnp.where(c == 0, u * SIDE + ring(w, dw), ring(w, dw) * SIDE + u)
                    pl.semaphore_signal(
                        barrier, inc=1, device_id=(own, ring(x, dx) * 2 + cc), device_id_type=MESH
                    )
                    greeted += 1
    for du in range(1, SIDE):
        pl.semaphore_signal(barrier, inc=1, device_id=at(x, w, ring(u, du), c), device_id_type=MESH)
        greeted += 1

    for k in range(tiles * slots):
        pltpu.make_async_copy(
            amp_ref.at[k // slots, k % slots], amp_vm.at[k], amp_sem.at[k]
        ).start()
    lane = lax.broadcasted_iota(I32, (8, 128), 1)
    row = lax.broadcasted_iota(I32, (8, 128), 0)
    listed = jnp.zeros((8, 128), I32)
    for t in range(tiles):
        for s in range(slots):
            own, loc = owner_ref[t, s], local_ref[t, s]
            used = counts_ref[t] > s
            none = per_owner * SIDE * SIDE
            straight = jnp.where(used, own * per_owner + loc, none)
            crossed = jnp.where(
                used, ((own % SIDE) * SIDE + own // SIDE) * per_owner + loc, none
            )
            here = lane == t * slots + s
            listed = jnp.where(here & (row == 0), straight, listed)
            listed = jnp.where(here & (row == 1), crossed, listed)
    meta_vm[...] = listed
    panels[per_owner * SIDE * SIDE] = jnp.zeros((cols, panel_ref.shape[2]), BF16)

    pl.semaphore_wait(barrier, greeted)

    def my_rows(ww):
        return panel_ref.at[:, pl.ds(pl.multiple_of(ww * cols, cols), cols), :]

    def place(uu, ww):
        return panels.at[pl.ds((uu * SIDE + ww) * per_owner, per_owner)]

    own_panel = pltpu.make_async_copy(my_rows(w), place(u, w), panel_own)
    own_panel.start()
    for dw in (1, 3, 2):
        pltpu.make_async_remote_copy(
            src_ref=my_rows(ring(w, dw)),
            dst_ref=place(u, w),
            send_sem=panel_send,
            recv_sem=panel_first.at[dw],
            device_id=at(x, ring(w, dw), u, c),
            device_id_type=MESH,
        ).start()

    half = slots // 2

    def handler(i):
        dw, h, k = i // 8, (i // 4) % 2, i % 4
        dx = jnp.where(k == 0, HOPS[0], jnp.where(k == 1, HOPS[1], jnp.where(k == 2, HOPS[2], HOPS[3])))
        xx = ring(x, dx)
        ww = ring(jnp.where(h == 0, z, y), dw)
        uu = jnp.where(h == 0, y, z)
        own = (dw == 0) & (dx == 0) & (h == c)
        col = (2 * xx + h) * (SIDE * cols) + ww * cols
        slot = (dw * SIDE + dx) * 2 + c
        return own, at(xx, ww, uu, h), col, slot

    def send_piece(r):
        t, s = r // 2, (r % 2) * half

        def one(i, _):
            own, device, col, slot = handler(i)
            src = amp_ref.at[t, pl.ds(s, half), :, pl.ds(pl.multiple_of(col, cols), cols)]
            dst = arrived.at[slot, t, pl.ds(s, half)]

            @pl.when(own)
            def _():
                pltpu.make_async_copy(src, dst, arrive_sem.at[slot, r]).start()

            @pl.when(jnp.logical_not(own))
            def _():
                pltpu.make_async_remote_copy(
                    src_ref=src,
                    dst_ref=dst,
                    send_sem=send_sem,
                    recv_sem=arrive_sem.at[slot, r],
                    device_id=device,
                    device_id_type=MESH,
                ).start()

            return 0

        lax.fori_loop(0, 32, one, 0)

    def send_meta(i, _):
        own, device, _, slot = handler(i)

        @pl.when(own)
        def _():
            pltpu.make_async_copy(meta_vm, meta_in.at[slot], meta_sem.at[slot]).start()

        @pl.when(jnp.logical_not(own))
        def _():
            pltpu.make_async_remote_copy(
                src_ref=meta_vm,
                dst_ref=meta_in.at[slot],
                send_sem=meta_send,
                recv_sem=meta_sem.at[slot],
                device_id=device,
                device_id_type=MESH,
            ).start()

        return 0

    send_piece(0)
    lax.fori_loop(0, 32, send_meta, 0)

    order = lax.broadcasted_iota(I32, (side, side), 0)
    source = lax.broadcasted_iota(I32, (side, side), 1)
    sort = (source == 2 * (order % (side // 2)) + order // (side // 2)).astype(BF16)
    zero = jnp.zeros((side, side), BF16)

    def prepare(n, _):
        f = fock_ref[n]
        top = jnp.concatenate([f, zero], axis=1)
        low = jnp.concatenate([zero, f], axis=1)
        fock_right[n] = jnp.concatenate([top, low], axis=0)
        g = jnp.dot(sort, f, preferred_element_type=F32).astype(BF16)
        g = lax.dot_general(g, sort, (((1,), (1,)), ((), ())), preferred_element_type=F32)
        fock_left[n] = g.astype(BF16)
        return 0

    lax.fori_loop(0, fock_ref.shape[0], prepare, 0)

    chunks = width // cols
    low_half = lax.broadcasted_iota(I32, (chunks, cols), 1) < side

    def residual(k, _):
        t, s = k // slots, k % slots
        pltpu.make_async_copy(amp_ref.at[t, s], amp_vm.at[k], amp_sem.at[k]).wait()
        ident = map_ref[owner_ref[t, s] * per_owner + local_ref[t, s]]
        used = counts_ref[t] > s
        row_tile = ident // fock_ref.shape[0]
        col_tile = ident % fock_ref.shape[0]
        for j in range(chunks):
            spread[pl.ds(j, rows, stride=chunks), :] = amp_vm[k, :, j * cols : (j + 1) * cols].astype(F32)
        for q in range(rows // 2):
            a = spread[2 * q * chunks : (2 * q + 1) * chunks, :]
            b = spread[(2 * q + 1) * chunks : (2 * q + 2) * chunks, :]
            even = jnp.where(low_half, a, pltpu.roll(b, side, 1))
            odd = jnp.where(low_half, pltpu.roll(a, side, 1), b)
            turned[:, q * cols : (q + 1) * cols] = jnp.concatenate([even, odd], axis=0).astype(BF16)
        left = jnp.dot(fock_left[row_tile], turned[...], preferred_element_type=F32)
        for q in range(rows // 2):
            even = left[:chunks, q * cols : (q + 1) * cols]
            odd = left[chunks:, q * cols : (q + 1) * cols]
            spread[2 * q * chunks : (2 * q + 1) * chunks, :] = jnp.where(
                low_half, even, pltpu.roll(odd, side, 1)
            )
            spread[(2 * q + 1) * chunks : (2 * q + 2) * chunks, :] = jnp.where(
                low_half, pltpu.roll(even, side, 1), odd
            )
        weight = hole_ref[t]
        right = fock_right[col_tile]
        for j in range(chunks):
            block = amp_vm[k, :, j * cols : (j + 1) * cols]
            total = jnp.dot(weight, block, preferred_element_type=F32)
            total += jnp.dot(block, right, preferred_element_type=F32)
            total += spread[pl.ds(j, rows, stride=chunks), :]
            out_vm[k, :, j * cols : (j + 1) * cols] = jnp.where(used, total, 0.0).astype(BF16)
        pltpu.make_async_copy(out_vm.at[k], res_ref.at[t, s], out_sem).start()
        return 0

    def pass_panels(ww):
        for du in (1, 3, 2):
            pltpu.make_async_remote_copy(
                src_ref=place(u, ww),
                dst_ref=place(u, ww),
                send_sem=panel_send,
                recv_sem=panel_second.at[du, ring(ww, SIDE - w)],
                device_id=at(x, w, ring(u, du), c),
                device_id_type=MESH,
            ).start()

    own_panel.wait()
    pass_panels(w)
    for dw in (1, 3, 2):
        there = place(u, ring(w, SIDE - dw))
        pltpu.make_async_copy(there, there, panel_first.at[dw]).wait()
        pass_panels(ring(w, SIDE - dw))
    send_piece(1)
    lax.fori_loop(0, 8, residual, 0)
    send_piece(2)
    send_piece(3)
    lax.fori_loop(8, 16, residual, 0)

    for dw in range(SIDE):
        for du in range(1, SIDE):
            there = place(ring(u, SIDE - du), ring(w, dw))
            pltpu.make_async_copy(there, there, panel_second.at[du, dw]).wait()

    def wait_meta(slot, _):
        pltpu.make_async_copy(meta_vm, meta_in.at[slot], meta_sem.at[slot]).wait()
        return 0

    lax.fori_loop(0, 32, wait_meta, 0)
    pltpu.sync_copy(meta_in, meta_sm)

    def ladder(slot, t, h):
        r = t * 2 + h
        there = arrived.at[slot, t, pl.ds(h * half, half)]
        pltpu.make_async_copy(there, there, arrive_sem.at[slot, r]).wait()
        blocks, weights = [], []
        for s in range(h * half, (h + 1) * half):
            blocks.append(arrived[slot, t, s])
            weights.append(panels[meta_sm[slot, c, t * slots + s]])
        return jnp.dot(
            jnp.concatenate(blocks, axis=1),
            jnp.concatenate(weights, axis=0),
            preferred_element_type=F32,
        )

    def first_half(t):
        def one(slot, _):
            part[t, slot] = ladder(slot, t, 0)
            return 0

        lax.fori_loop(0, 32, one, 0)

    def second_half(t):
        def one(slot, _):
            part[t, slot] += ladder(slot, t, 1)
            return 0

        for dw in (2, 1, 3, 0):
            lax.fori_loop(dw * 8, dw * 8 + 8, one, 0)
            if dw:
                pltpu.make_async_remote_copy(
                    src_ref=part.at[t, pl.ds(dw * 8, 8)],
                    dst_ref=part_in.at[t, dw - 1],
                    send_sem=part_send,
                    recv_sem=part_sem.at[t, dw - 1],
                    device_id=at(x, ring(w, SIDE - dw), u, c),
                    device_id_type=MESH,
                ).start()

    def send_home(t):
        for dw in range(1, SIDE):
            there = part_in.at[t, dw - 1]
            pltpu.make_async_copy(there, there, part_sem.at[t, dw - 1]).wait()
        for k in (2, 3, 6, 7, 4, 5, 0, 1):
            dx, core = k // 2, k % 2
            ring_sum[t, k] = (
                part[t, k] + part_in[t, 0, k] + part_in[t, 1, k] + part_in[t, 2, k]
            )
            src, dst, sem = ring_sum.at[t, k], home_in.at[t, c, dx], home_sem.at[t, c, dx]

            def far(src=src, dst=dst, sem=sem, dx=dx, core=core):
                pltpu.make_async_remote_copy(
                    src_ref=src,
                    dst_ref=dst,
                    send_sem=home_send,
                    recv_sem=sem,
                    device_id=(occ, ring(x, SIDE - dx) * 2 + core),
                    device_id_type=MESH,
                ).start()

            if dx:
                far()
            else:
                pl.when(c != core)(far)

                @pl.when(c == core)
                def _(src=src, dst=dst, sem=sem):
                    pltpu.make_async_copy(src, dst, sem).start()

    def finish(t):
        total = jnp.zeros(lad_ref.shape[1:], F32)
        for h in range(2):
            for dx in range(SIDE):
                there = home_in.at[t, h, dx]
                pltpu.make_async_copy(there, there, home_sem.at[t, h, dx]).wait()
                total = total + home_in[t, h, dx]
        lad_ref[t] = total.astype(BF16)

    first_half(0)
    second_half(0)
    first_half(1)
    send_home(0)
    second_half(1)
    finish(0)
    send_home(1)
    finish(1)

    def drained(ref, sem):
        pltpu.make_async_copy(ref, ref, sem).wait()

    drained(amp_ref.at[:, :, :, pl.ds(0, width - cols)], send_sem)
    drained(meta_in.at[pl.ds(0, 31)], meta_send)
    drained(panels.at[pl.ds(0, 15 * per_owner)], panel_send)
    drained(part_in, part_send)
    drained(home_in.at[:, 0], home_send)
    drained(home_in.at[:, 0, pl.ds(0, 3)], home_send)
    drained(out_vm, out_sem)


def per_device(
    amplitudes,
    tile_counts,
    tile_owner,
    tile_local,
    pair_map,
    hole_weight,
    fock_tiles,
    ladder_panels,
):
    tiles, slots, rows, width = amplitudes.shape
    per_owner, depth, panel = ladder_panels.shape
    tile_count, side, _ = fock_tiles.shape
    cols = 128
    dma = pltpu.SemaphoreType.DMA
    smem, vmem, hbm = (pl.BlockSpec(memory_space=m) for m in (pltpu.SMEM, pltpu.VMEM, pl.ANY))
    flops = 2 * tiles * slots * rows * width * (3 * side + panel)
    return pl.pallas_call(
        body,
        out_shape=(
            jax.ShapeDtypeStruct(amplitudes.shape, BF16),
            jax.ShapeDtypeStruct((tiles, rows, panel), BF16),
        ),
        in_specs=[smem, smem, smem, smem, hbm, vmem, vmem, hbm],
        out_specs=(hbm, vmem),
        scratch_shapes=[
            pltpu.VMEM((tiles * slots, rows, width), BF16),
            pltpu.VMEM((tiles * slots, rows, width), BF16),
            pltpu.VMEM((32, tiles, slots, rows, cols), BF16),
            pltpu.VMEM((16 * per_owner + 1, cols, panel), BF16),
            pltpu.VMEM((8, 128), I32),
            pltpu.VMEM((32, 8, 128), I32),
            pltpu.SMEM((32, 8, 128), I32),
            pltpu.VMEM((tiles, 32, rows, panel), F32),
            pltpu.VMEM((tiles, 3, 8, rows, panel), F32),
            pltpu.VMEM((tiles, 8, rows, panel), F32),
            pltpu.VMEM((tiles, 2, SIDE, rows, panel), F32),
            pltpu.VMEM((tile_count, 2 * side, 2 * side), BF16),
            pltpu.VMEM((tile_count, side, side), BF16),
            pltpu.VMEM((rows * width // cols, cols), F32),
            pltpu.VMEM((side, rows * width // side), BF16),
            dma((tiles * slots,)),
            dma(()),
            dma(()),
            dma((32, 4)),
            dma(()),
            dma((32,)),
            dma(()),
            dma(()),
            dma((SIDE,)),
            dma((SIDE, SIDE)),
            dma(()),
            dma((tiles, 3)),
            dma(()),
            dma((tiles, 2, SIDE)),
        ],
        compiler_params=pltpu.CompilerParams(
            collective_id=0, has_side_effects=True, vmem_limit_bytes=60 << 20
        ),
        cost_estimate=pl.CostEstimate(
            flops=flops, bytes_accessed=4 * tiles * slots * rows * width, transcendentals=0
        ),
    )(
        tile_counts,
        tile_owner,
        tile_local,
        pair_map,
        amplitudes,
        hole_weight,
        fock_tiles,
        ladder_panels,
    )


def solution(mesh):
    in_specs = (
        P(("occ", "vir"), None, None, None),
        P(("occ", "vir")),
        P(("occ", "vir"), None),
        P(("occ", "vir"), None),
        P(),
        P(("occ", "vir"), None, None),
        P(),
        P("occ", "vir", None),
    )
    out_specs = (P(("occ", "vir"), None, None, None), P(("occ", "vir"), None, None))
    return jax.shard_map(
        per_device, mesh=mesh, in_specs=in_specs, out_specs=out_specs, check_vma=False
    )
```

time: 432 us -> 157 us (0.36)
  Pallas kernels: 0 us -> 147 us
  waiting for transfers between devices: 133 us -> 0 us
  matrix products: 123 us -> 0 us
  local copies, waits for them, and re-layouts: 118 us -> 8.51 us
  starting transfers between devices: 28 us -> 0 us
  between operations: 14.1 us -> 0.65 us
  other arithmetic: 11.3 us -> 0 us
    pallas_call x0 -> x1, Pallas kernels: none -> 147 us  [per_device(): pl.pallas_call(body, out_shape=(jax.ShapeDtypeStruct(amplitudes.shape, BF...]
    all_to_all x3 -> x0, waiting for transfers between devices: 133 us -> none  [the longest x1 133 us: per_device(): lax.all_to_all(outgoing, 'occ', split_axis=0, concat_axis=0, tiled=True)]
    dot_general x7 -> x0, matrix products: 123 us -> none  [the longest x1 32.5 us: per_device(): jnp.einsum('ocpn,ocnq->ocpq', arrived, chosen, preferred_element_type=jnp...]
    reshape x3 -> x0, local copies, waits for them, and re-layouts: 51.7 us -> none  [the longest x1 27.9 us: per_device(): fock_part.reshape(local_tiles, slot_count, pair_rows, tile_size)]
    add x1 -> x0, local copies, waits for them, and re-layouts: 31.1 us -> none  [per_device(): fock_part + jnp.einsum('Psce,Psped->Pspcd', left_fock, shaped, preferred_...]
    all_to_all x3 -> x0, starting transfers between devices: 28 us -> none  [the longest x1 12.6 us: per_device(): lax.all_to_all(partial_value, 'occ', split_axis=0, concat_axis=0, tiled=T...]
    scatter x2 -> x0, local copies, waits for them, and re-layouts: 22.6 us -> none  [the longest x1 22 us: per_device(): jnp.zeros((owners * CAP, pair_rows, tile_size), jnp.bfloat16).at[send_index]]
    select_n x4 -> x0, other arithmetic: 9.29 us -> none  [the longest x1 8.49 us: per_device(): jnp.where(used_slot[:, :, None, None], amplitudes, jnp.zeros((), jnp.bflo...]
  transfers between devices with their start and end apart: 4 -> 0, of which waited for: 2 -> 0; matrix products, arithmetic and copies ran while one was open for 50% -> 0% of each run, Pallas kernels for 0% -> 0%
where the time goes in v1:
time: 157 us; the launch traced here: 156 us
  Pallas kernels  147 us (94%)
  local copies, waits for them, and re-layouts  8.51 us (5%)
    pallas_call x1, Pallas kernels, per_device(): pl.pallas_call(body, out_shape=(jax.ShapeDtypeStruct(amplitudes.shape, BF...  147 us
    unnamed x4, local copies, waits for them, and re-layouts  8.51 us

profile of v1, /device:TPU:1, one launch (start us, length us, event | category | flops | bytes accessed | tf_op | source)
XLA Modules:
  0.0 155.9 jit_solution(18143764311820649083)
XLA Ops:
  0.6 146.7 %shard_map.95 = (bf16[2,8,64,4096]{3,2,1,0:T(8,128)(2,1)}, bf16[2,64,128]{2,1,0:T(8,128)(2,1)}) custom-call(s32[2]{0:T(128)} %counts_ref.1, s32[2,8]{1,0:T(2,128)} %owner_ref.1, s32[2,8]{1,0:T(2,128)} %local_ref.1, s32[256]{0:T(256)} %map_ref.1, bf16[2,8,64,4096]{3,2,1,0:T(8,128)(2,1)} %amp_ref.1, bf16[2,64,64]{2,1,0:T(8,128)(2,1)} %hole_ref.1, ...), custom_call_target="tpu_custom_call" | custom-call | flops 2684354560 | bytes 16777216 | tf_op jit(solution)/shard_map/pallas_call | solution.py:401
  147.3 0.0 copy-start
  147.3 7.9 %copy.12 = bf16[2,8,64,4096]{3,2,1,0:T(8,128)(2,1)} copy(bf16[2,8,64,4096]{3,2,1,0:T(8,128)(2,1)} %get-tuple-element.4) | data formatting | bytes 16777216
  155.2 0.0 copy-done
  155.2 0.6 copy.13
Async XLA Ops:
  147.3 7.9 %copy-start = (bf16[2,64,128]{2,1,0:T(8,128)(2,1)S(1)}, bf16[2,64,128]{2,1,0:T(8,128)(2,1)}, u32[]{:S(2)}) copy-start(bf16[2,64,128]{2,1,0:T(8,128)(2,1)} %get-tuple-element.5) | copy-start | bytes 98308

commit v2 on v1

--- a/solution.py
+++ b/solution.py
@@ -11,6 +11,7 @@
 SIDE = 4
 BF16, F32, I32 = jnp.bfloat16, jnp.float32, jnp.int32
 HOPS = (1, 3, 2, 0)
+RINGS = (2, 1, 3, 0)
 
 
 def body(
@@ -25,7 +26,6 @@
     res_ref,
     lad_ref,
     amp_vm,
-    out_vm,
     arrived,
     panels,
     meta_vm,
@@ -40,7 +40,6 @@
     spread,
     turned,
     amp_sem,
-    out_sem,
     send_sem,
     arrive_sem,
     meta_send,
@@ -49,6 +48,7 @@
     panel_own,
     panel_first,
     panel_second,
+    panel_third,
     part_send,
     part_sem,
     home_send,
@@ -129,11 +129,77 @@
             device_id_type=MESH,
         ).start()
 
+    part_tiles = per_owner // 2
+
+    def place_part(uu, ww, p):
+        return panels.at[pl.ds((uu * SIDE + ww) * per_owner + p * part_tiles, part_tiles)]
+
+    def pass_panels(dw, p, du):
+        there = place_part(u, ring(w, dw), p)
+        held = panel_ref.at[
+            pl.ds(p * part_tiles, part_tiles), pl.ds(pl.multiple_of(w * cols, cols), cols), :
+        ]
+        pltpu.make_async_remote_copy(
+            src_ref=there if dw else held,
+            dst_ref=there,
+            send_sem=panel_send,
+            recv_sem=panel_second.at[dw, p, du // 2],
+            device_id=at(x, w, ring(u, du), c),
+            device_id_type=MESH,
+        ).start()
+
+    def wait_neighbour(dw, p, du):
+        there = place_part(ring(u, SIDE - du), ring(w, dw), p)
+        pltpu.make_async_copy(there, there, panel_second.at[dw, p, du // 2]).wait()
+
+    def pass_on(dw, p):
+        du = 1 if p == 0 else SIDE - 1
+        there = place_part(ring(u, SIDE - du), ring(w, dw), p)
+        pltpu.make_async_remote_copy(
+            src_ref=there,
+            dst_ref=there,
+            send_sem=panel_send,
+            recv_sem=panel_third.at[dw, p],
+            device_id=at(x, w, ring(u, du), c),
+            device_id_type=MESH,
+        ).start()
+
+    def wait_first(dw):
+        there = place(u, ring(w, dw))
+        pltpu.make_async_copy(there, there, panel_first.at[SIDE - dw]).wait()
+
+    def second(dw):
+        if dw:
+            wait_first(dw)
+        for p, du in ((0, 1), (1, 3), (1, 1), (0, 3)):
+            pass_panels(dw, p, du)
+
+    def third(dw):
+        wait_neighbour(dw, 0, 1)
+        pass_on(dw, 0)
+        wait_neighbour(dw, 1, 3)
+        pass_on(dw, 1)
+
+    def all_panels():
+        own_panel.wait()
+        for dw in range(SIDE):
+            wait_neighbour(dw, 1, 1)
+            wait_neighbour(dw, 0, 3)
+            for p in range(2):
+                there = place_part(ring(u, 2), ring(w, dw), p)
+                pltpu.make_async_copy(there, there, panel_third.at[dw, p]).wait()
+
+    second(0)
+
     half = slots // 2
 
     def handler(i):
-        dw, h, k = i // 8, (i // 4) % 2, i % 4
-        dx = jnp.where(k == 0, HOPS[0], jnp.where(k == 1, HOPS[1], jnp.where(k == 2, HOPS[2], HOPS[3])))
+        def pick(k, table):
+            return jnp.where(
+                k == 0, table[0], jnp.where(k == 1, table[1], jnp.where(k == 2, table[2], table[3]))
+            )
+
+        dw, h, dx = pick(i // 8, RINGS), (i // 4) % 2, pick(i % 4, HOPS)
         xx = ring(x, dx)
         ww = ring(jnp.where(h == 0, z, y), dw)
         uu = jnp.where(h == 0, y, z)
@@ -142,7 +208,7 @@
         slot = (dw * SIDE + dx) * 2 + c
         return own, at(xx, ww, uu, h), col, slot
 
-    def send_piece(r):
+    def send_piece(r, first=0, last=32):
         t, s = r // 2, (r % 2) * half
 
         def one(i, _):
@@ -167,7 +233,7 @@
 
             return 0
 
-        lax.fori_loop(0, 32, one, 0)
+        lax.fori_loop(first, last, one, 0)
 
     def send_meta(i, _):
         own, device, _, slot = handler(i)
@@ -244,38 +310,22 @@
             total = jnp.dot(weight, block, preferred_element_type=F32)
             total += jnp.dot(block, right, preferred_element_type=F32)
             total += spread[pl.ds(j, rows, stride=chunks), :]
-            out_vm[k, :, j * cols : (j + 1) * cols] = jnp.where(used, total, 0.0).astype(BF16)
-        pltpu.make_async_copy(out_vm.at[k], res_ref.at[t, s], out_sem).start()
+            res_ref[t, s, :, j * cols : (j + 1) * cols] = jnp.where(used, total, 0.0).astype(BF16)
         return 0
 
-    def pass_panels(ww):
-        for du in (1, 3, 2):
-            pltpu.make_async_remote_copy(
-                src_ref=place(u, ww),
-                dst_ref=place(u, ww),
-                send_sem=panel_send,
-                recv_sem=panel_second.at[du, ring(ww, SIDE - w)],
-                device_id=at(x, w, ring(u, du), c),
-                device_id_type=MESH,
-            ).start()
-
-    own_panel.wait()
-    pass_panels(w)
-    for dw in (1, 3, 2):
-        there = place(u, ring(w, SIDE - dw))
-        pltpu.make_async_copy(there, there, panel_first.at[dw]).wait()
-        pass_panels(ring(w, SIDE - dw))
+    lax.fori_loop(0, 2, residual, 0)
+    third(0)
+    for dw in (3, 1, 2):
+        second(dw)
     send_piece(1)
-    lax.fori_loop(0, 8, residual, 0)
+    lax.fori_loop(2, 9, residual, 0)
+    for dw in (3, 1, 2):
+        third(dw)
     send_piece(2)
+    lax.fori_loop(9, 13, residual, 0)
     send_piece(3)
-    lax.fori_loop(8, 16, residual, 0)
-
-    for dw in range(SIDE):
-        for du in range(1, SIDE):
-            there = place(ring(u, SIDE - du), ring(w, dw))
-            pltpu.make_async_copy(there, there, panel_second.at[du, dw]).wait()
-
+    lax.fori_loop(13, 16, residual, 0)
+    all_panels()
     def wait_meta(slot, _):
         pltpu.make_async_copy(meta_vm, meta_in.at[slot], meta_sem.at[slot]).wait()
         return 0
@@ -309,7 +359,7 @@
             part[t, slot] += ladder(slot, t, 1)
             return 0
 
-        for dw in (2, 1, 3, 0):
+        for dw in RINGS:
             lax.fori_loop(dw * 8, dw * 8 + 8, one, 0)
             if dw:
                 pltpu.make_async_remote_copy(
@@ -378,7 +428,6 @@
     drained(part_in, part_send)
     drained(home_in.at[:, 0], home_send)
     drained(home_in.at[:, 0, pl.ds(0, 3)], home_send)
-    drained(out_vm, out_sem)
 
 
 def per_device(
@@ -401,13 +450,12 @@
     return pl.pallas_call(
         body,
         out_shape=(
-            jax.ShapeDtypeStruct(amplitudes.shape, BF16),
+            pltpu.VMEM(amplitudes.shape, BF16),
             jax.ShapeDtypeStruct((tiles, rows, panel), BF16),
         ),
         in_specs=[smem, smem, smem, smem, hbm, vmem, vmem, hbm],
-        out_specs=(hbm, vmem),
+        out_specs=(vmem, vmem),
         scratch_shapes=[
-            pltpu.VMEM((tiles * slots, rows, width), BF16),
             pltpu.VMEM((tiles * slots, rows, width), BF16),
             pltpu.VMEM((32, tiles, slots, rows, cols), BF16),
             pltpu.VMEM((16 * per_owner + 1, cols, panel), BF16),
@@ -424,21 +472,21 @@
             pltpu.VMEM((side, rows * width // side), BF16),
             dma((tiles * slots,)),
             dma(()),
-            dma(()),
             dma((32, 4)),
             dma(()),
             dma((32,)),
             dma(()),
             dma(()),
             dma((SIDE,)),
-            dma((SIDE, SIDE)),
+            dma((SIDE, 2, 2)),
+            dma((SIDE, 2)),
             dma(()),
             dma((tiles, 3)),
             dma(()),
             dma((tiles, 2, SIDE)),
         ],
         compiler_params=pltpu.CompilerParams(
-            collective_id=0, has_side_effects=True, vmem_limit_bytes=60 << 20
+            collective_id=0, has_side_effects=True, vmem_limit_bytes=54 << 20
         ),
         cost_estimate=pl.CostEstimate(
             flops=flops, bytes_accessed=4 * tiles * slots * rows * width, transcendentals=0

time: 157 us -> 136 us (0.87)
  Pallas kernels: 147 us -> 131 us
  local copies, waits for them, and re-layouts: 8.51 us -> 4.02 us
    pallas_call x1, Pallas kernels: 147 us -> 131 us  [per_device(): pl.pallas_call(body, out_shape=(pltpu.VMEM(amplitudes.shape, BF16), jax.S...]
    unnamed x4, local copies, waits for them, and re-layouts: 8.51 us -> 4.02 us
where the time goes in v2:
time: 136 us
  Pallas kernels  131 us (96%)
  local copies, waits for them, and re-layouts  4.02 us (3%)
    pallas_call x1, Pallas kernels, per_device(): pl.pallas_call(body, out_shape=(pltpu.VMEM(amplitudes.shape, BF16), jax.S...  131 us
    unnamed x4, local copies, waits for them, and re-layouts  4.02 us

profile of v2, /device:TPU:1, one launch (start us, length us, event | category | flops | bytes accessed | tf_op | source)
XLA Modules:
  0.0 135.7 jit_solution(3253827643684584037)
XLA Ops:
  0.6 131.1 %shard_map.95 = (bf16[2,8,64,4096]{3,2,1,0:T(8,128)(2,1)S(1)}, bf16[2,64,128]{2,1,0:T(8,128)(2,1)}) custom-call(s32[2]{0:T(128)} %counts_ref.1, s32[2,8]{1,0:T(2,128)} %owner_ref.1, s32[2,8]{1,0:T(2,128)} %local_ref.1, s32[256]{0:T(256)} %map_ref.1, bf16[2,8,64,4096]{3,2,1,0:T(8,128)(2,1)} %amp_ref.1, bf16[2,64,64]{2,1,0:T(8,128)(2,1)} %hole_ref.1, ...), custom_call_target="tpu_custom_call" | custom-call | flops 2684354560 | bytes 16777216 | tf_op jit(solution)/shard_map/pallas_call | solution.py:450
  131.7 0.0 copy-start
  131.7 3.4 %copy.12 = bf16[2,8,64,4096]{3,2,1,0:T(8,128)(2,1)} copy(bf16[2,8,64,4096]{3,2,1,0:T(8,128)(2,1)S(1)} %get-tuple-element.2) | data formatting | bytes 16777216
  135.1 0.0 copy-done
  135.1 0.6 copy.13
Async XLA Ops:
  131.7 3.4 %copy-start = (bf16[2,64,128]{2,1,0:T(8,128)(2,1)S(1)}, bf16[2,64,128]{2,1,0:T(8,128)(2,1)}, u32[]{:S(2)}) copy-start(bf16[2,64,128]{2,1,0:T(8,128)(2,1)} %get-tuple-element.7) | copy-start | bytes 98308

commit v3 on v2

--- a/solution.py
+++ b/solution.py
@@ -11,7 +11,7 @@
 SIDE = 4
 BF16, F32, I32 = jnp.bfloat16, jnp.float32, jnp.int32
 HOPS = (1, 3, 2, 0)
-RINGS = (2, 1, 3, 0)
+RINGS = (0, 2, 1, 3)
 
 
 def body(
@@ -68,6 +68,11 @@
         own = jnp.where(core == 0, uu * SIDE + ww, ww * SIDE + uu)
         return (own, xx * 2 + core)
 
+    def pick(k, table):
+        return jnp.where(
+            k == 0, table[0], jnp.where(k == 1, table[1], jnp.where(k == 2, table[2], table[3]))
+        )
+
     def ring(v, d):
         return lax.rem(v + d + SIDE, SIDE)
 
@@ -194,11 +199,6 @@
     half = slots // 2
 
     def handler(i):
-        def pick(k, table):
-            return jnp.where(
-                k == 0, table[0], jnp.where(k == 1, table[1], jnp.where(k == 2, table[2], table[3]))
-            )
-
         dw, h, dx = pick(i // 8, RINGS), (i // 4) % 2, pick(i % 4, HOPS)
         xx = ring(x, dx)
         ww = ring(jnp.where(h == 0, z, y), dw)
@@ -255,8 +255,11 @@
 
         return 0
 
-    send_piece(0)
     lax.fori_loop(0, 32, send_meta, 0)
+    send_piece(0, 0, 8)
+    send_piece(1, 0, 8)
+    send_piece(2, 0, 8)
+    send_piece(3, 0, 8)
 
     order = lax.broadcasted_iota(I32, (side, side), 0)
     source = lax.broadcasted_iota(I32, (side, side), 1)
@@ -313,17 +316,18 @@
             res_ref[t, s, :, j * cols : (j + 1) * cols] = jnp.where(used, total, 0.0).astype(BF16)
         return 0
 
-    lax.fori_loop(0, 2, residual, 0)
+    lax.fori_loop(0, 4, residual, 0)
     third(0)
     for dw in (3, 1, 2):
         second(dw)
-    send_piece(1)
-    lax.fori_loop(2, 9, residual, 0)
+    send_piece(0, 8, 32)
+    lax.fori_loop(4, 9, residual, 0)
     for dw in (3, 1, 2):
         third(dw)
-    send_piece(2)
+    send_piece(1, 8, 32)
     lax.fori_loop(9, 13, residual, 0)
-    send_piece(3)
+    send_piece(2, 8, 32)
+    send_piece(3, 8, 32)
     lax.fori_loop(13, 16, residual, 0)
     all_panels()
     def wait_meta(slot, _):
@@ -333,43 +337,52 @@
     lax.fori_loop(0, 32, wait_meta, 0)
     pltpu.sync_copy(meta_in, meta_sm)
 
-    def ladder(slot, t, h):
-        r = t * 2 + h
-        there = arrived.at[slot, t, pl.ds(h * half, half)]
-        pltpu.make_async_copy(there, there, arrive_sem.at[slot, r]).wait()
-        blocks, weights = [], []
-        for s in range(h * half, (h + 1) * half):
-            blocks.append(arrived[slot, t, s])
-            weights.append(panels[meta_sm[slot, c, t * slots + s]])
-        return jnp.dot(
-            jnp.concatenate(blocks, axis=1),
-            jnp.concatenate(weights, axis=0),
-            preferred_element_type=F32,
-        )
-
-    def first_half(t):
-        def one(slot, _):
-            part[t, slot] = ladder(slot, t, 0)
+    def ladder(dw, t, first, last):
+        group = dw * 8
+        for r in range(first // half, last // half):
+
+            def wait_slot(k, _, r=r):
+                there = arrived.at[group + k, t, pl.ds(r * half, half)]
+                pltpu.make_async_copy(there, there, arrive_sem.at[group + k, t * 2 + r]).wait()
+                return 0
+
+            lax.fori_loop(0, 8, wait_slot, 0)
+        sums = []
+        for k in range(8):
+            blocks = [arrived[group + k, t, s] for s in range(first, last)]
+            weights = [panels[meta_sm[group + k, c, t * slots + s]] for s in range(first, last)]
+            sums.append(
+                jnp.dot(
+                    jnp.concatenate(blocks, axis=1),
+                    jnp.concatenate(weights, axis=0),
+                    preferred_element_type=F32,
+                )
+            )
+        for k in range(8):
+            if first == 0:
+                part[t, group + k] = sums[k]
+            else:
+                part[t, group + k] += sums[k]
+
+    def pass_sums(dw, t):
+        pltpu.make_async_remote_copy(
+            src_ref=part.at[t, pl.ds(dw * 8, 8)],
+            dst_ref=part_in.at[t, dw - 1],
+            send_sem=part_send,
+            recv_sem=part_sem.at[t, dw - 1],
+            device_id=at(x, ring(w, SIDE - dw), u, c),
+            device_id_type=MESH,
+        ).start()
+
+    def part_of_list(t, first, last):
+        def one(g, _):
+            dw = pick(g, RINGS)
+            ladder(dw, t, first, last)
+            if last == slots:
+                pl.when(dw > 0)(lambda: pass_sums(dw, t))
             return 0
 
-        lax.fori_loop(0, 32, one, 0)
-
-    def second_half(t):
-        def one(slot, _):
-            part[t, slot] += ladder(slot, t, 1)
-            return 0
-
-        for dw in RINGS:
-            lax.fori_loop(dw * 8, dw * 8 + 8, one, 0)
-            if dw:
-                pltpu.make_async_remote_copy(
-                    src_ref=part.at[t, pl.ds(dw * 8, 8)],
-                    dst_ref=part_in.at[t, dw - 1],
-                    send_sem=part_send,
-                    recv_sem=part_sem.at[t, dw - 1],
-                    device_id=at(x, ring(w, SIDE - dw), u, c),
-                    device_id_type=MESH,
-                ).start()
+        lax.fori_loop(0, SIDE, one, 0)
 
     def send_home(t):
         for dw in range(1, SIDE):
@@ -410,11 +423,10 @@
                 total = total + home_in[t, h, dx]
         lad_ref[t] = total.astype(BF16)
 
-    first_half(0)
-    second_half(0)
-    first_half(1)
+    part_of_list(0, 0, slots)
+    part_of_list(1, 0, half)
     send_home(0)
-    second_half(1)
+    part_of_list(1, half, slots)
     finish(0)
     send_home(1)
     finish(1)

time: 136 us -> 131 us (0.963)
  Pallas kernels: 131 us -> 126 us
    pallas_call x1, Pallas kernels: 131 us -> 126 us  [per_device(): pl.pallas_call(body, out_shape=(pltpu.VMEM(amplitudes.shape, BF16), jax.S...]
where the time goes in v3:
time: 131 us
  Pallas kernels  126 us (96%)
  local copies, waits for them, and re-layouts  4.02 us (3%)
    pallas_call x1, Pallas kernels, per_device(): pl.pallas_call(body, out_shape=(pltpu.VMEM(amplitudes.shape, BF16), jax.S...  126 us
    unnamed x4, local copies, waits for them, and re-layouts  4.02 us

profile of v3, /device:TPU:1, one launch (start us, length us, event | category | flops | bytes accessed | tf_op | source)
XLA Modules:
  0.0 130.8 jit_solution(8119176124282952741)
XLA Ops:
  0.6 126.2 %shard_map.95 = (bf16[2,8,64,4096]{3,2,1,0:T(8,128)(2,1)S(1)}, bf16[2,64,128]{2,1,0:T(8,128)(2,1)}) custom-call(s32[2]{0:T(128)} %counts_ref.1, s32[2,8]{1,0:T(2,128)} %owner_ref.1, s32[2,8]{1,0:T(2,128)} %local_ref.1, s32[256]{0:T(256)} %map_ref.1, bf16[2,8,64,4096]{3,2,1,0:T(8,128)(2,1)} %amp_ref.1, bf16[2,64,64]{2,1,0:T(8,128)(2,1)} %hole_ref.1, ...), custom_call_target="tpu_custom_call" | custom-call | flops 2684354560 | bytes 16777216 | tf_op jit(solution)/shard_map/pallas_call | solution.py:462
  126.8 0.0 copy-start
  126.8 3.4 %copy.12 = bf16[2,8,64,4096]{3,2,1,0:T(8,128)(2,1)} copy(bf16[2,8,64,4096]{3,2,1,0:T(8,128)(2,1)S(1)} %get-tuple-element.2) | data formatting | bytes 16777216
  130.2 0.0 copy-done
  130.2 0.6 copy.13
Async XLA Ops:
  126.8 3.4 %copy-start = (bf16[2,64,128]{2,1,0:T(8,128)(2,1)S(1)}, bf16[2,64,128]{2,1,0:T(8,128)(2,1)}, u32[]{:S(2)}) copy-start(bf16[2,64,128]{2,1,0:T(8,128)(2,1)} %get-tuple-element.7) | copy-start | bytes 98308

commit v4 on v3

--- a/solution.py
+++ b/solution.py
@@ -35,6 +35,7 @@
     part_in,
     ring_sum,
     home_in,
+    direct_in,
     fock_right,
     fock_left,
     spread,
@@ -53,6 +54,7 @@
     part_sem,
     home_send,
     home_sem,
+    direct_sem,
 ):
     tiles, slots, rows, width = amp_ref.shape
     per_owner = panel_ref.shape[0]
@@ -90,6 +92,13 @@
                     greeted += 1
     for du in range(1, SIDE):
         pl.semaphore_signal(barrier, inc=1, device_id=at(x, w, ring(u, du), c), device_id_type=MESH)
+        greeted += 1
+
+    for dx in range(SIDE):
+        far = jnp.where(c == 0, ring(y, 3) * SIDE + z, y * SIDE + ring(z, 3))
+        pl.semaphore_signal(
+            barrier, inc=1, device_id=(far, ring(x, dx) * 2 + 1 - c), device_id_type=MESH
+        )
         greeted += 1
 
     for k in range(tiles * slots):
@@ -374,7 +383,7 @@
             device_id_type=MESH,
         ).start()
 
-    def part_of_list(t, first, last):
+    def part_of_list(t, first, last, groups=SIDE):
         def one(g, _):
             dw = pick(g, RINGS)
             ladder(dw, t, first, last)
@@ -382,17 +391,28 @@
                 pl.when(dw > 0)(lambda: pass_sums(dw, t))
             return 0
 
-        lax.fori_loop(0, SIDE, one, 0)
+        lax.fori_loop(0, groups, one, 0)
+
+    def send_direct(t):
+        for k in range(8):
+            dx, core = k // 2, k % 2
+            pltpu.make_async_remote_copy(
+                src_ref=part.at[t, 24 + k],
+                dst_ref=direct_in.at[c, dx],
+                send_sem=part_send,
+                recv_sem=direct_sem.at[c, dx],
+                device_id=(at(x, ring(w, 1), u, c)[0], ring(x, SIDE - dx) * 2 + core),
+                device_id_type=MESH,
+            ).start()
 
     def send_home(t):
-        for dw in range(1, SIDE):
+        for dw in range(1, SIDE if t == 0 else 3):
             there = part_in.at[t, dw - 1]
             pltpu.make_async_copy(there, there, part_sem.at[t, dw - 1]).wait()
         for k in (2, 3, 6, 7, 4, 5, 0, 1):
             dx, core = k // 2, k % 2
-            ring_sum[t, k] = (
-                part[t, k] + part_in[t, 0, k] + part_in[t, 1, k] + part_in[t, 2, k]
-            )
+            total = part[t, k] + part_in[t, 0, k] + part_in[t, 1, k]
+            ring_sum[t, k] = total + part_in[t, 2, k] if t == 0 else total
             src, dst, sem = ring_sum.at[t, k], home_in.at[t, c, dx], home_sem.at[t, c, dx]
 
             def far(src=src, dst=dst, sem=sem, dx=dx, core=core):
@@ -421,13 +441,19 @@
                 there = home_in.at[t, h, dx]
                 pltpu.make_async_copy(there, there, home_sem.at[t, h, dx]).wait()
                 total = total + home_in[t, h, dx]
+                if t == 1:
+                    there = direct_in.at[h, dx]
+                    pltpu.make_async_copy(there, there, direct_sem.at[h, dx]).wait()
+                    total = total + direct_in[h, dx]
         lad_ref[t] = total.astype(BF16)
 
     part_of_list(0, 0, slots)
     part_of_list(1, 0, half)
     send_home(0)
-    part_of_list(1, half, slots)
+    part_of_list(1, half, slots, SIDE - 1)
     finish(0)
+    ladder(RINGS[3], 1, half, slots)
+    send_direct(1)
     send_home(1)
     finish(1)
 
@@ -478,6 +504,7 @@
             pltpu.VMEM((tiles, 3, 8, rows, panel), F32),
             pltpu.VMEM((tiles, 8, rows, panel), F32),
             pltpu.VMEM((tiles, 2, SIDE, rows, panel), F32),
+            pltpu.VMEM((2, SIDE, rows, panel), F32),
             pltpu.VMEM((tile_count, 2 * side, 2 * side), BF16),
             pltpu.VMEM((tile_count, side, side), BF16),
             pltpu.VMEM((rows * width // cols, cols), F32),
@@ -496,6 +523,7 @@
             dma((tiles, 3)),
             dma(()),
             dma((tiles, 2, SIDE)),
+            dma((2, SIDE)),
         ],
         compiler_params=pltpu.CompilerParams(
             collective_id=0, has_side_effects=True, vmem_limit_bytes=54 << 20

time: 131 us -> 131 us (level)
  no operation moved by 1% of the time
where the time goes in v4:
time: 131 us
  Pallas kernels  126 us (96%)
  local copies, waits for them, and re-layouts  4.02 us (3%)
    pallas_call x1, Pallas kernels, per_device(): pl.pallas_call(body, out_shape=(pltpu.VMEM(amplitudes.shape, BF16), jax.S...  126 us
    unnamed x4, local copies, waits for them, and re-layouts  4.02 us

profile of v4, /device:TPU:1, one launch (start us, length us, event | category | flops | bytes accessed | tf_op | source)
XLA Modules:
  0.0 130.7 jit_solution(6736874904388966410)
XLA Ops:
  0.6 126.0 %shard_map.95 = (bf16[2,8,64,4096]{3,2,1,0:T(8,128)(2,1)S(1)}, bf16[2,64,128]{2,1,0:T(8,128)(2,1)}) custom-call(s32[2]{0:T(128)} %counts_ref.1, s32[2,8]{1,0:T(2,128)} %owner_ref.1, s32[2,8]{1,0:T(2,128)} %local_ref.1, s32[256]{0:T(256)} %map_ref.1, bf16[2,8,64,4096]{3,2,1,0:T(8,128)(2,1)} %amp_ref.1, bf16[2,64,64]{2,1,0:T(8,128)(2,1)} %hole_ref.1, ...), custom_call_target="tpu_custom_call" | custom-call | flops 2684354560 | bytes 16777216 | tf_op jit(solution)/shard_map/pallas_call | solution.py:488
  126.6 0.0 copy-start
  126.6 3.4 %copy.12 = bf16[2,8,64,4096]{3,2,1,0:T(8,128)(2,1)} copy(bf16[2,8,64,4096]{3,2,1,0:T(8,128)(2,1)S(1)} %get-tuple-element.2) | data formatting | bytes 16777216
  130.0 0.0 copy-done
  130.0 0.6 copy.13
Async XLA Ops:
  126.6 3.4 %copy-start = (bf16[2,64,128]{2,1,0:T(8,128)(2,1)S(1)}, bf16[2,64,128]{2,1,0:T(8,128)(2,1)}, u32[]{:S(2)}) copy-start(bf16[2,64,128]{2,1,0:T(8,128)(2,1)} %get-tuple-element.7) | copy-start | bytes 98308
